TPU v7x, 32 devices: a whole 2x2x4 slice. The times are simulated.
32 devices in a mesh: groups: 2 (over y), dom: 4 (over z), blk: 4 (over x, core).
Axes of the slice: x: 2, y: 2, z: 4, core: 2. Of those that a mesh axis runs over, the one named last changes fastest.
Arguments:
- features: bfloat16 [16384, 128], P(('groups', 'dom', 'blk')), parts along dimension 0, may hold values from -6 to 6
- weight: bfloat16 [128, 256], replicated, may hold values from -0.5 to 0.5
- tiles: bfloat16 [8, 4, 19, 128, 128], P(('groups', 'dom'), 'blk'), parts along dimension 0, may hold values from -0.25 to 0.25
- tile_rows: int32 [8, 4, 19], P(('groups', 'dom'), 'blk'), parts along dimension 0, may hold values from 0 to 15
- tile_sources: int32 [8, 4, 19], P(('groups', 'dom'), 'blk'), parts along dimension 0, may hold values from 0 to 7, as said below
- send_blocks: int32 [8, 4, 4], P(('groups', 'dom'), 'blk'), parts along dimension 0, may hold values from 0 to 4, as said below
- cotangent: bfloat16 [16384, 256], P(('groups', 'dom', 'blk')), parts along dimension 0, may hold values from -6 to 6
Outputs:
- activations: bfloat16 [16384, 256], P(('groups', 'dom', 'blk')), parts along dimension 0
- feature_grad: bfloat16 [16384, 128], P(('groups', 'dom', 'blk')), parts along dimension 0
- weight_grad: float32 [256, 256], P('groups'), parts along dimension 0
There are 2 independent parts, one for each index of `groups`. A program takes and returns all parts, laid end to end along the dimension named above; an argument that names none is the same for every part. Nothing has to cross between parts.
Inputs may be any that keep to these rules, and one draw needn't show every extreme that they name: `send_blocks`: entry [e, b, d] names the row block of device (e, b) that domain d reads, counted within that device's 4 blocks; 4 means none. Entry [d, b, d] is always 4. A domain reads from at most 3 other domains. `tile_sources`: slot s below 4 is the device's own s-th row block; slot 4 + e is the block received from domain e and is named only where send_blocks[e, b, d] is below 4; every such received block is named by at least one tile of the reader.
All inputs are finite; a program needn't handle non-finite values.
Results may differ from a plain program's by a relative error of at most 0.0063.
Values may be sent and summed in bfloat16 or wider, within the bound.
A program may use at most 64 MiB of HBM per device.

v0:
```python
import math

import jax
import jax.numpy as jnp
from jax import lax
from jax.sharding import PartitionSpec as P


def per_device(features, weight, tiles, tile_rows, tile_sources, send_blocks, cotangent):
    domains = lax.axis_size("dom")
    members = lax.axis_size("blk")
    tile_size = tiles.shape[-1]
    own_count = features.shape[0] // tile_size
    hidden = weight.shape[1]
    projected = jnp.dot(features, weight, preferred_element_type=jnp.float32).astype(jnp.bfloat16)
    own_blocks = projected.reshape(own_count, tile_size, hidden)
    chosen = send_blocks[0, 0]
    picker = chosen[:, None] == jnp.arange(own_count)[None, :]
    outgoing = jnp.einsum(
        "er,rih->eih", picker.astype(jnp.bfloat16), own_blocks, preferred_element_type=jnp.float32
    ).astype(jnp.bfloat16)
    received = lax.all_to_all(outgoing, "dom", split_axis=0, concat_axis=0, tiled=True)
    slots = jnp.concatenate([own_blocks, received], axis=0)
    sources = tile_sources[0, 0]
    targets = tile_rows[0, 0]
    tile_mats = tiles[0, 0]
    gathered = jnp.take(slots, sources, axis=0)
    contrib = jnp.einsum("tij,tjh->tih", tile_mats, gathered, preferred_element_type=jnp.float32)
    dom_rows = own_count * members
    partial_value = jnp.zeros((dom_rows, tile_size, hidden), jnp.float32).at[targets].add(contrib)
    aggregated = lax.psum_scatter(
        partial_value.reshape(dom_rows * tile_size, hidden), "blk", scatter_dimension=0, tiled=True
    )
    activations = jax.nn.silu(aggregated).astype(jnp.bfloat16)
    sigmoid_z = jax.nn.sigmoid(aggregated)
    pre_grad = (
        cotangent.astype(jnp.float32) * sigmoid_z * (1.0 + aggregated * (1.0 - sigmoid_z))
    ).astype(jnp.bfloat16)
    domain_grad = lax.all_gather(pre_grad, "blk", axis=0, tiled=True).reshape(
        dom_rows, tile_size, hidden
    )
    target_grads = jnp.take(domain_grad, targets, axis=0)
    back = jnp.einsum("tji,tjh->tih", tile_mats, target_grads, preferred_element_type=jnp.float32)
    slot_sums = (
        jnp.zeros((own_count + domains, tile_size, hidden), jnp.float32).at[sources].add(back)
    )
    halo_terms = slot_sums[own_count:].astype(jnp.bfloat16)
    returned = lax.all_to_all(halo_terms, "dom", split_axis=0, concat_axis=0, tiled=True)
    usable = chosen < own_count
    landing = jnp.where(usable, chosen, own_count)
    padded_own = jnp.concatenate(
        [slot_sums[:own_count], jnp.zeros((1, tile_size, hidden), jnp.float32)], axis=0
    )
    own_grad = padded_own.at[landing].add(returned.astype(jnp.float32))[:own_count]
    projected_grad = own_grad.reshape(own_count * tile_size, hidden).astype(jnp.bfloat16)
    partial_weight = lax.dot_general(
        features, projected_grad, (((0,), (0,)), ((), ())), preferred_element_type=jnp.float32
    )
    node_total = own_count * tile_size * domains * members
    weight_grad = lax.psum(partial_weight, ("dom", "blk")) / math.sqrt(node_total)
    feature_grad = lax.dot_general(
        projected_grad, weight, (((1,), (1,)), ((), ())), preferred_element_type=jnp.float32
    ).astype(jnp.bfloat16)
    return (activations, feature_grad, weight_grad)


def solution(mesh):
    return jax.shard_map(
        per_device,
        mesh=mesh,
        in_specs=(
            P(("groups", "dom", "blk"), None),
            P(),
            P(("groups", "dom"), "blk", None, None, None),
            P(("groups", "dom"), "blk", None),
            P(("groups", "dom"), "blk", None),
            P(("groups", "dom"), "blk", None),
            P(("groups", "dom", "blk"), None),
        ),
        out_specs=(
            P(("groups", "dom", "blk"), None),
            P(("groups", "dom", "blk"), None),
            P("groups", None),
        ),
        check_vma=False,
    )
```

profile of v0, /device:TPU:0, one launch (start us, length us, event | category | flops | bytes accessed | tf_op | source)
XLA Modules:
  0.0 211.3 jit_solution(15120577428795894064)
XLA Ops:
  7.2 0.0 copy-start
  7.2 0.0 copy-start.6
  7.2 0.0 copy-start.7
  7.2 1.2 convolution_convert_fusion
  8.4 1.0 fusion.8
  9.4 0.7 copy.25
  10.1 6.3 %all-to-all-start = ((bf16[4,128,256]{2,1,0:T(8,128)(2,1)}), bf16[4,128,256]{2,1,0:T(8,128)(2,1)S(1)}, u32[]{:S(2)}, u32[]{:S(2)}) async-start(bf16[4,128,256]{2,1,0:T(8,128)(2,1)} %copy.25), calls=%async_computation | async-start | bytes 524288 | tf_op jit(solution)/shard_map/all_to_all | solution.py:22
  16.4 0.0 reduce-scatter.2.cloned.1.call-start
  16.4 0.0 copy-done.6
  16.5 0.0 copy-done.7
  16.5 8.9 %all-to-all-done = bf16[4,128,256]{2,1,0:T(8,128)(2,1)S(1)} async-done(((bf16[4,128,256]{2,1,0:T(8,128)(2,1)}), bf16[4,128,256]{2,1,0:T(8,128)(2,1)S(1)}, u32[]{:S(2)}, u32[]{:S(2)}) %all-to-all-start) | async-done | bytes 262176 | tf_op jit(solution)/shard_map/all_to_all | solution.py:22
  25.4 1.8 gather_fusion
  27.2 0.0 copy-done
  27.2 1.9 convolution_bitcast_fusion.1
  29.1 2.1 copy.14
  31.2 0.2 broadcast_in_dim.31
  31.4 5.9 %scatter_fusion = f32[16,128,256]{2,1,0:T(8,128)S(1)} fusion(f32[16,128,256]{2,1,0:T(8,128)S(1)} %broadcast_in_dim.31, s32[19]{0:T(128)S(1)} %fusion.13, f32[19,128,256]{2,1,0:T(8,128)} %copy.14), kind=kCustom, calls=%fused_computation.2 | custom fusion | flops 622592 | bytes 7471180 | tf_op jit(solution)/shard_map/scatter-add | solution.py:30
  37.2 0.0 copy-start.1
  37.2 0.0 copy-start.3
  37.3 1.3 copy-done.1
  38.6 0.0 reduce-scatter.2.cloned.1.call-update
  38.6 0.0 all-gather.2.cloned.1.call-start
  38.7 30.6 %reduce-scatter.2.cloned.1.call-done = f32[512,256]{1,0:T(8,128)} async-done(((f32[2048,256]{1,0:T(8,128)}), f32[512,256]{1,0:T(8,128)}) %reduce-scatter.2.cloned.1.call-update) | async-done | bytes 524304 | tf_op jit(solution)/shard_map/reduce_scatter | solution.py:31
  69.3 2.1 multiply_convert_fusion
  71.3 0.0 all-gather.2.cloned.1.call-update
  71.4 16.9 %all-gather.2.cloned.1.call-done = bf16[2048,256]{1,0:T(8,128)(2,1)} async-done(((bf16[512,256]{1,0:T(8,128)(2,1)}), bf16[2048,256]{1,0:T(8,128)(2,1)}) %all-gather.2.cloned.1.call-update) | async-done | bytes 1048592 | tf_op jit(solution)/shard_map/all_gather | solution.py:39
  88.2 3.0 %gather_fusion.1 = bf16[19,128,256]{2,1,0:T(8,128)(2,1)} fusion(bf16[16,128,256]{2,1,0:T(8,128)(2,1)} %bitcast.44, s32[1024]{0:T(1024)S(1)} %pad_clamp_fusion), kind=kCustom, calls=%fused_computation.1 | custom fusion | bytes 2490444 | tf_op jit(solution)/shard_map/jit(_take)/gather | solution.py:42
  91.2 1.9 convolution_bitcast_fusion
  93.1 2.1 copy.16
  95.2 0.1 broadcast_in_dim.34
  95.3 0.0 copy-start.8
  95.3 0.0 copy-start.5
  95.3 5.8 %scatter_fusion.1 = f32[8,128,256]{2,1,0:T(8,128)S(1)} fusion(f32[8,128,256]{2,1,0:T(8,128)S(1)} %broadcast_in_dim.34, s32[19]{0:T(128)S(1)} %fusion.14, f32[19,128,256]{2,1,0:T(8,128)} %copy.16), kind=kCustom, calls=%fused_computation.3 | custom fusion | flops 622592 | bytes 7471180 | tf_op jit(solution)/shard_map/scatter-add | solution.py:45
  101.2 0.7 slice.26
  101.9 4.6 %all-to-all-start.1 = ((bf16[4,128,256]{2,1,0:T(8,128)(2,1)}), bf16[4,128,256]{2,1,0:T(8,128)(2,1)S(1)}, u32[]{:S(2)}, u32[]{:S(2)}) async-start(bf16[4,128,256]{2,1,0:T(8,128)(2,1)} %slice.26), calls=%async_computation.2 | async-start | bytes 524288 | tf_op jit(solution)/shard_map/all_to_all | solution.py:48
  106.5 0.0 copy-done.5
  106.5 0.1 slice_select_fusion
  106.7 9.2 %all-to-all-done.1 = bf16[4,128,256]{2,1,0:T(8,128)(2,1)S(1)} async-done(((bf16[4,128,256]{2,1,0:T(8,128)(2,1)}), bf16[4,128,256]{2,1,0:T(8,128)(2,1)S(1)}, u32[]{:S(2)}, u32[]{:S(2)}) %all-to-all-start.1) | async-done | bytes 262176 | tf_op jit(solution)/shard_map/all_to_all | solution.py:48
  115.9 0.0 copy-start.2
  115.9 0.0 copy-start.4
  115.9 0.9 scatter_fusion.2
  116.8 0.0 copy-done.2
  116.8 0.9 convolution_bitcast_fusion.2
  117.7 0.0 all-reduce.2.cloned.1.call-update
  117.8 0.9 convolution_convert_fusion.1
  118.7 84.4 %all-reduce.2.cloned.1.call-done = f32[128,256]{0,1:T(8,128)} async-done(((f32[128,256]{0,1:T(8,128)}), f32[128,256]{0,1:T(8,128)}) %all-reduce.2.cloned.1.call-update) | async-done | bytes 131088 | tf_op jit(solution)/shard_map/psum | solution.py:60
  203.1 0.9 broadcast_multiply_fusion
  204.0 0.8 copy.17
  (14 shorter events, 0.2 us)
Async XLA Ops:
  7.2 20.0 %copy-start = (bf16[1,1,19,128,128]{4,3,2,1,0:T(8,128)(2,1)S(1)}, bf16[1,1,19,128,128]{4,3,2,1,0:T(8,128)(2,1)}, u32[]{:S(2)}) copy-start(bf16[1,1,19,128,128]{4,3,2,1,0:T(8,128)(2,1)} %param.9) | copy-start | bytes 1867780
  7.2 9.3 %copy-start.6 = (s32[1,1,19]{2,1,0:T(1,128)S(1)}, s32[1,1,19]{2,1,0:T(1,128)}, u32[]{:S(2)}) copy-start(s32[1,1,19]{2,1,0:T(1,128)} %param.11) | copy-start | bytes 232
  7.2 9.3 %copy-start.7 = (s32[1,1,19]{2,1,0:T(1,128)S(1)}, s32[1,1,19]{2,1,0:T(1,128)}, u32[]{:S(2)}) copy-start(s32[1,1,19]{2,1,0:T(1,128)} %param.10) | copy-start | bytes 232
  10.1 15.2 %all-to-all-start = ((bf16[4,128,256]{2,1,0:T(8,128)(2,1)}), bf16[4,128,256]{2,1,0:T(8,128)(2,1)S(1)}, u32[]{:S(2)}, u32[]{:S(2)}) async-start(bf16[4,128,256]{2,1,0:T(8,128)(2,1)} %copy.25), calls=%async_computation | async-start | bytes 524288 | tf_op jit(solution)/shard_map/all_to_all | solution.py:22
  16.4 52.8 %reduce-scatter.2.cloned.1.call-start = ((), (), s32[]{:S(2)}) async-start(), calls=%async_computation.3 | async-start | bytes 2621440 | tf_op jit(solution)/shard_map/reduce_scatter | solution.py:31
  37.2 1.3 copy-start.1
  37.2 32.0 %copy-start.3 = (bf16[512,256]{1,0:T(8,128)(2,1)S(1)}, bf16[512,256]{1,0:T(8,128)(2,1)}, u32[]{:S(2)}) copy-start(bf16[512,256]{1,0:T(8,128)(2,1)} %param.13) | copy-start | bytes 786436
  38.6 49.6 %all-gather.2.cloned.1.call-start = ((), (), s32[]{:S(2)}) async-start(), calls=%async_computation.4 | async-start | bytes 1310720 | tf_op jit(solution)/shard_map/all_gather | solution.py:39
  95.3 11.2 %copy-start.8 = (s32[1,1,4]{2,1,0:T(1,128)S(1)}, s32[1,1,4]{2,1,0:T(1,128)}, u32[]{:S(2)}) copy-start(s32[1,1,4]{2,1,0:T(1,128)} %param.12) | copy-start | bytes 52
  95.3 11.2 %copy-start.5 = (pred[5]{0:T(512)(128)(4,1)S(1)}, pred[5]{0:T(512)(128)(4,1)}, u32[]{:S(2)}) copy-start(pred[5]{0:T(512)(128)(4,1)} %constant.29.clone.1) | copy-start | bytes 19
  101.9 13.9 %all-to-all-start.1 = ((bf16[4,128,256]{2,1,0:T(8,128)(2,1)}), bf16[4,128,256]{2,1,0:T(8,128)(2,1)S(1)}, u32[]{:S(2)}, u32[]{:S(2)}) async-start(bf16[4,128,256]{2,1,0:T(8,128)(2,1)} %slice.26), calls=%async_computation.2 | async-start | bytes 524288 | tf_op jit(solution)/shard_map/all_to_all | solution.py:48
  106.5 96.6 %all-reduce.2.cloned.1.call-start = ((), (), s32[]{:S(2)}) async-start(), calls=%async_computation.5 | async-start | bytes 262144 | tf_op jit(solution)/shard_map/psum | solution.py:60
  115.9 0.9 copy-start.2
  115.9 1.9 copy-start.4
Sparse Core Ops, SparseCore 0:
  38.7 30.4 reduce-scatter.1
  71.5 16.7 all-gather.1
  117.9 85.1 all-reduce.1
where the time goes:
time: 213 us; the launch traced here: 211 us
  waiting for transfers between devices  150 us (70%)
  other arithmetic  15.8 us (7%)
  between operations  14 us (7%)
  local copies, waits for them, and re-layouts  12.8 us (6%)
  starting transfers between devices  11 us (5%)
  matrix products  7.79 us (4%)
    psum x1, waiting for transfers between devices, per_device(): lax.psum(partial_weight, ('dom', 'blk')) / math.sqrt(node_total)  84.4 us
    reduce_scatter x1, waiting for transfers between devices, per_device(): lax.psum_scatter(partial_value.reshape(dom_rows * tile_size, hidden), 'bl...  30.6 us
    all_gather x1, waiting for transfers between devices, per_device(): lax.all_gather(pre_grad, 'blk', axis=0, tiled=True)  16.9 us
    all_to_all x1, waiting for transfers between devices, per_device(): lax.all_to_all(halo_terms, 'dom', split_axis=0, concat_axis=0, tiled=True)  9.16 us
    all_to_all x1, waiting for transfers between devices, per_device(): lax.all_to_all(outgoing, 'dom', split_axis=0, concat_axis=0, tiled=True)  8.85 us
    all_to_all x1, starting transfers between devices, per_device(): lax.all_to_all(outgoing, 'dom', split_axis=0, concat_axis=0, tiled=True)  6.32 us
    scatter-add x1, other arithmetic, per_device(): jnp.zeros((dom_rows, tile_size, hidden), jnp.float32).at[targets]  5.86 us
    scatter-add x1, other arithmetic, per_device(): jnp.zeros((own_count + domains, tile_size, hidden), jnp.float32).at[sources]  5.84 us
  transfers between devices with their start and end apart: 5, of which 5 were waited for; matrix products, arithmetic and copies ran while one was open for 0% of the time, Pallas kernels for 0%

commit v1 on v0

v1 whole, which is shorter than its diff:
```python
import functools
import math

import jax
import jax.numpy as jnp
from jax import lax
from jax.experimental import pallas as pl
from jax.experimental.pallas import tpu as pltpu
from jax.sharding import PartitionSpec as P

MESH = pl.DeviceIdType.MESH
BF16 = jnp.bfloat16
F32 = jnp.float32
DMA = pltpu.SemaphoreType.DMA


def each(low, high, step):
    if high - low <= 16:
        for i in range(low, high):
            step(i)
    else:
        lax.fori_loop(low, high, lambda i, c: (step(i), c)[1], 0)


def chain(keys, key_count, none):
    before = []
    for t, key in enumerate(keys):
        found = none
        for u in range(t):
            found = jnp.where(keys[u] == key, u, found)
        before.append(found)
    last = []
    for r in range(key_count):
        found = none
        for t, key in enumerate(keys):
            found = jnp.where(key == r, t, found)
        last.append(found)
    return before, last


def kernel(
    domains, members, sum_here, scale,
    rows_ref, sources_ref, chosen_ref, feat_hbm, weight_hbm, tiles_hbm, cot_hbm,
    act_hbm, fgrad_hbm, wgrad_hbm,
    feat, weight, tiles, tiles_t, cot, slots, outgoing, acc, last_ref, rs_out, rs_in, act, dom_h,
    ret_out, ret_in, fgrad, wpart, wparts, wgrad,
    local_sem, halo_send, halo_recv, rs_send, rs_recv, ag_send, ag_recv, ret_send, ret_recv,
    ws_send, ws_recv, wg_send, wg_recv,
):
    own, size, width = feat.shape
    count = tiles.shape[0]
    d = lax.axis_index("dom")
    b = lax.axis_index("blk")
    peers = domains * members
    me = d * members + b

    def dom_at(k):
        return lax.rem(d + k, domains)

    def blk_at(k):
        return lax.rem(b + k, members)

    def peer_at(k):
        index = lax.rem(me + k, peers)
        return index, {"dom": index // members, "blk": lax.rem(index, members)}

    loads = [
        pltpu.make_async_copy(feat_hbm, feat, local_sem.at[0]),
        pltpu.make_async_copy(feat_hbm, slots.at[pl.ds(0, own)], local_sem.at[1]),
        pltpu.make_async_copy(tiles_hbm.at[0, 0], tiles, local_sem.at[2]),
        pltpu.make_async_copy(weight_hbm, weight, local_sem.at[3]),
        pltpu.make_async_copy(cot_hbm, cot, local_sem.at[4]),
    ]
    for load in loads:
        load.start()

    barrier = pltpu.get_barrier_semaphore()
    if sum_here:
        each(1, peers, lambda k: pl.semaphore_signal(
            barrier, inc=1, device_id=peer_at(k)[1], device_id_type=MESH))
        waits = peers - 1
    else:
        each(1, domains, lambda k: pl.semaphore_signal(
            barrier, inc=1, device_id={"dom": dom_at(k)}, device_id_type=MESH))
        each(1, members, lambda k: pl.semaphore_signal(
            barrier, inc=1, device_id={"blk": blk_at(k)}, device_id_type=MESH))
        waits = domains + members - 2

    loads[0].wait()

    def pick(k):
        outgoing[k - 1] = feat[jnp.minimum(chosen_ref[0, 0, dom_at(k)], own - 1)]

    each(1, domains, pick)
    pl.semaphore_wait(barrier, waits)

    def halo(k):
        return pltpu.make_async_remote_copy(
            outgoing.at[k - 1], slots.at[own + d], halo_send.at[k - 1], halo_recv.at[k - 1],
            device_id={"dom": dom_at(k)}, device_id_type=MESH)

    def halo_in(k):
        return pltpu.make_async_remote_copy(
            outgoing.at[k - 1], slots.at[own + dom_at(domains - k)], halo_send.at[k - 1],
            halo_recv.at[k - 1], device_id={"dom": dom_at(k)}, device_id_type=MESH)

    each(1, domains, lambda k: halo(k).start())

    rows = [rows_ref[0, 0, t] for t in range(count)]
    sources = [sources_ref[0, 0, t] for t in range(count)]
    before, last = chain(rows, own * members, count)
    for r, value in enumerate(last):
        last_ref[r] = value
    acc[count] = jnp.zeros((size, width), F32)
    slots[own + d] = jnp.zeros((size, width), BF16)
    for load in loads[1:]:
        load.wait()
    each(1, domains, lambda k: halo_in(k).wait_recv())

    for t in range(count):
        product = jnp.dot(tiles[t], slots[sources[t]], preferred_element_type=F32)
        acc[t] = product + acc[before[t]]

    def scatter(m):
        return pltpu.make_async_remote_copy(
            rs_out.at[m - 1], rs_in.at[m - 1], rs_send.at[m - 1], rs_recv.at[m - 1],
            device_id={"blk": blk_at(m)}, device_id_type=MESH)

    for m in range(1, members):
        target = blk_at(m)
        for s in range(own):
            rs_out[m - 1, s] = acc[last_ref[target * own + s]].astype(BF16)
        scatter(m).start()

    own_rows = [acc[last_ref[b * own + s]] for s in range(own)]
    total = jnp.concatenate(own_rows, axis=0)

    before, last = chain(sources, own + domains, count)
    for t in range(count):
        tiles_t[t] = tiles[t].T

    for m in range(1, members):
        scatter(m).wait_recv()
        total = total + rs_in[m - 1].reshape(own * size, width).astype(F32)

    gathered = total.astype(BF16)
    z = jnp.dot(gathered, weight[...], preferred_element_type=F32)
    sig = jax.nn.sigmoid(z)
    grad = (cot[...].astype(F32) * sig * (1.0 + z * (1.0 - sig))).astype(BF16)
    h = lax.dot_general(
        grad, weight[...], (((1,), (1,)), ((), ())), preferred_element_type=F32).astype(BF16)
    dom_h[pl.ds(b * own, own)] = h.reshape(own, size, width)

    def spread(m):
        return pltpu.make_async_remote_copy(
            dom_h.at[pl.ds(b * own, own)], dom_h.at[pl.ds(b * own, own)], ag_send.at[m - 1],
            ag_recv.at[m - 1], device_id={"blk": blk_at(m)}, device_id_type=MESH)

    def spread_in(m):
        return pltpu.make_async_remote_copy(
            dom_h.at[pl.ds(b * own, own)], dom_h.at[pl.ds(blk_at(members - m) * own, own)],
            ag_send.at[m - 1], ag_recv.at[m - 1], device_id={"blk": blk_at(m)},
            device_id_type=MESH)

    for m in range(1, members):
        spread(m).start()

    act[...] = (z * sig).astype(BF16)
    stores = [pltpu.make_async_copy(act, act_hbm, local_sem.at[5])]
    stores[0].start()
    wpart[...] = lax.dot_general(
        gathered, grad, (((0,), (0,)), ((), ())), preferred_element_type=F32)
    piece = wpart.shape[0] // peers

    def wscatter(k):
        index, device = peer_at(k)
        return pltpu.make_async_remote_copy(
            wpart.at[pl.ds(pl.multiple_of(index * piece, 8), piece)], wparts.at[k - 1],
            ws_send.at[k - 1], ws_recv.at[k - 1], device_id=device, device_id_type=MESH)

    def wspread(k, who):
        piece_at = pl.ds(pl.multiple_of(who * piece, 8), piece)
        return pltpu.make_async_remote_copy(
            wgrad.at[piece_at], wgrad.at[piece_at], wg_send.at[k - 1], wg_recv.at[k - 1],
            device_id=peer_at(k)[1], device_id_type=MESH)

    if sum_here:
        each(1, peers, lambda k: wscatter(k).start())
    else:
        wgrad[...] = wpart[...] * scale

    for m in range(1, members):
        spread_in(m).wait_recv()
    for t in range(count):
        product = jnp.dot(tiles_t[t], dom_h[rows[t]], preferred_element_type=F32)
        acc[t] = product + acc[before[t]]
    for s, value in enumerate(last):
        last_ref[s] = value

    def give_back(k):
        return pltpu.make_async_remote_copy(
            ret_out.at[k - 1], ret_in.at[k - 1], ret_send.at[k - 1], ret_recv.at[k - 1],
            device_id={"dom": dom_at(k)}, device_id_type=MESH)

    def give(k):
        ret_out[k - 1] = acc[last_ref[own + dom_at(k)]].astype(BF16)
        give_back(k).start()

    each(1, domains, give)

    if sum_here:
        each(1, peers, lambda k: wscatter(k).wait_recv())
        mine = pl.ds(pl.multiple_of(me * piece, 8), piece)
        summed = wpart[mine, :]
        for k in range(1, peers):
            summed = summed + wparts[k - 1]
        wgrad[mine, :] = summed * scale
        each(1, peers, lambda k: wspread(k, me).start())

    for s in range(own):
        fgrad[s] = acc[last_ref[s]]

    def land(k):
        give_back(k).wait_recv()
        block = chosen_ref[0, 0, dom_at(domains - k)]
        value = ret_in[k - 1].astype(F32)
        for s in range(own):
            fgrad[s] += jnp.where(block == s, value, 0.0)

    each(1, domains, land)
    feat[...] = fgrad[...].astype(BF16)
    stores.append(pltpu.make_async_copy(feat, fgrad_hbm, local_sem.at[6]))
    stores[1].start()

    if sum_here:
        each(1, peers, lambda k: wspread(k, lax.rem(me + peers - k, peers)).wait_recv())
    stores.append(pltpu.make_async_copy(wgrad, wgrad_hbm, local_sem.at[7]))
    stores[2].start()

    each(1, domains, lambda k: halo(k).wait_send())
    each(1, domains, lambda k: give_back(k).wait_send())
    for m in range(1, members):
        scatter(m).wait_send()
        spread(m).wait_send()
    if sum_here:
        each(1, peers, lambda k: wscatter(k).wait_send())
        each(1, peers, lambda k: wspread(k, me).wait_send())
    for store in stores:
        store.wait()


def per_device(features, weight, tiles, tile_rows, tile_sources, send_blocks, cotangent):
    domains = lax.axis_size("dom")
    members = lax.axis_size("blk")
    peers = domains * members
    count, size = tiles.shape[2], tiles.shape[-1]
    own = features.shape[0] // size
    width, hidden = weight.shape
    nodes = own * size
    sum_here = width % (8 * peers) == 0
    scale = 1.0 / math.sqrt(nodes * peers)
    piece = width // peers if sum_here else 8
    pieces = peers - 1 if sum_here else 1
    halos = max(domains - 1, 1)
    others = max(members - 1, 1)
    vmem = pltpu.VMEM
    smem = pl.BlockSpec(memory_space=pltpu.SMEM)
    anywhere = pl.BlockSpec(memory_space=pl.ANY)
    activations, feature_grad, weight_grad = pl.pallas_call(
        functools.partial(kernel, domains, members, sum_here, scale),
        out_shape=(
            jax.ShapeDtypeStruct((nodes, hidden), BF16),
            jax.ShapeDtypeStruct((own, size, width), BF16),
            jax.ShapeDtypeStruct((width, hidden), F32),
        ),
        in_specs=[smem] * 3 + [anywhere] * 4,
        out_specs=(anywhere,) * 3,
        scratch_shapes=[
            vmem((own, size, width), BF16),
            vmem((width, hidden), BF16),
            vmem((count, size, size), BF16),
            vmem((count, size, size), BF16),
            vmem((nodes, hidden), BF16),
            vmem((own + domains, size, width), BF16),
            vmem((halos, size, width), BF16),
            vmem((count + 1, size, width), F32),
            pltpu.SMEM((max(own * members, own + domains),), jnp.int32),
            vmem((others, own, size, width), BF16),
            vmem((others, own, size, width), BF16),
            vmem((nodes, hidden), BF16),
            vmem((own * members, size, width), BF16),
            vmem((halos, size, width), BF16),
            vmem((halos, size, width), BF16),
            vmem((own, size, width), F32),
            vmem((width, hidden), F32),
            vmem((pieces, piece, hidden), F32),
            vmem((width, hidden), F32),
            DMA((8,)),
            DMA((halos,)), DMA((halos,)),
            DMA((others,)), DMA((others,)),
            DMA((others,)), DMA((others,)),
            DMA((halos,)), DMA((halos,)),
            DMA((pieces,)), DMA((pieces,)),
            DMA((pieces,)), DMA((pieces,)),
        ],
        compiler_params=pltpu.CompilerParams(
            collective_id=0, has_side_effects=True, vmem_limit_bytes=40 * 1024 * 1024),
    )(tile_rows, tile_sources, send_blocks, features.reshape(own, size, width), weight, tiles, cotangent)
    if not sum_here:
        weight_grad = lax.psum(weight_grad, ("dom", "blk"))
    return activations, feature_grad.reshape(nodes, width), weight_grad


def solution(mesh):
    return jax.shard_map(
        per_device,
        mesh=mesh,
        in_specs=(
            P(("groups", "dom", "blk"), None),
            P(),
            P(("groups", "dom"), "blk", None, None, None),
            P(("groups", "dom"), "blk", None),
            P(("groups", "dom"), "blk", None),
            P(("groups", "dom"), "blk", None),
            P(("groups", "dom", "blk"), None),
        ),
        out_specs=(
            P(("groups", "dom", "blk"), None),
            P(("groups", "dom", "blk"), None),
            P("groups", None),
        ),
        check_vma=False,
    )
```

time: 213 us -> 41.2 us (0.19)
  waiting for transfers between devices: 150 us -> 0 us
  Pallas kernels: 0 us -> 33.8 us
  other arithmetic: 15.8 us -> 0 us
  between operations: 14 us -> 0.67 us
  starting transfers between devices: 11 us -> 0 us
  matrix products: 7.79 us -> 0 us
  local copies, waits for them, and re-layouts: 12.8 us -> 6.45 us
    psum x1 -> x0, waiting for transfers between devices: 84.4 us -> none  [per_device(): lax.psum(partial_weight, ('dom', 'blk')) / math.sqrt(node_total)]
    pallas_call x0 -> x1, Pallas kernels: none -> 33.8 us  [per_device(): pl.pallas_call(functools.partial(kernel, domains, members, sum_here, scal...]
    reduce_scatter x1 -> x0, waiting for transfers between devices: 30.6 us -> none  [per_device(): lax.psum_scatter(partial_value.reshape(dom_rows * tile_size, hidden), 'bl...]
    all_to_all x2 -> x0, waiting for transfers between devices: 18 us -> none  [the longest x1 9.16 us: per_device(): lax.all_to_all(halo_terms, 'dom', split_axis=0, concat_axis=0, tiled=True)]
    all_gather x1 -> x0, waiting for transfers between devices: 16.9 us -> none  [per_device(): lax.all_gather(pre_grad, 'blk', axis=0, tiled=True)]
    scatter-add x3 -> x0, other arithmetic: 12.6 us -> none  [the longest x1 5.86 us: per_device(): jnp.zeros((dom_rows, tile_size, hidden), jnp.float32).at[targets]]
    all_to_all x2 -> x0, starting transfers between devices: 10.9 us -> none  [the longest x1 6.32 us: per_device(): lax.all_to_all(outgoing, 'dom', split_axis=0, concat_axis=0, tiled=True)]
    dot_general x6 -> x0, matrix products: 7.79 us -> none  [the longest x1 1.91 us: per_device(): jnp.einsum('tji,tjh->tih', tile_mats, target_grads, preferred_element_typ...]
  transfers between devices with their start and end apart: 5 -> 0, of which waited for: 5 -> 0; matrix products, arithmetic and copies ran while one was open for 0% -> 0% of each run, Pallas kernels for 0% -> 0%
where the time goes in v1:
time: 41.2 us; the launch traced here: 40.9 us
  Pallas kernels  33.8 us (82%)
  local copies, waits for them, and re-layouts  6.45 us (16%)
  between operations  0.67 us (2%)
    pallas_call x1, Pallas kernels, per_device(): pl.pallas_call(functools.partial(kernel, domains, members, sum_here, scal...  33.8 us
    unnamed x17, local copies, waits for them, and re-layouts  6.45 us

profile of v1, /device:TPU:0, one launch (start us, length us, event | category | flops | bytes accessed | tf_op | source)
XLA Modules:
  0.0 40.9 jit_solution(12848360452947105274)
XLA Ops:
  0.6 0.0 copy-start.6
  0.6 0.0 copy-start.5
  0.7 0.0 copy-start.4
  0.7 0.6 %copy-done.6 = s32[1,1,4]{2,1,0:T(1,128)S(1)} copy-done((s32[1,1,4]{2,1,0:T(1,128)S(1)}, s32[1,1,4]{2,1,0:T(1,128)}, u32[]{:S(2)}) %copy-start.6) | copy-done | bytes 40
  1.3 0.0 copy-done.5
  1.3 0.0 copy-done.4
  1.3 0.0 copy-start
  1.3 1.1 %copy-done = bf16[1,1,19,128,128]{4,3,2,1,0:T(8,128)(2,1)S(1)} copy-done((bf16[1,1,19,128,128]{4,3,2,1,0:T(8,128)(2,1)S(1)}, bf16[1,1,19,128,128]{4,3,2,1,0:T(8,128)(2,1)}, u32[]{:S(2)}) %copy-start) | copy-done | bytes 622616
  2.4 0.0 copy-start.1
  2.4 0.9 %copy-done.1 = bf16[512,256]{1,0:T(8,128)(2,1)S(1)} copy-done((bf16[512,256]{1,0:T(8,128)(2,1)S(1)}, bf16[512,256]{1,0:T(8,128)(2,1)}, u32[]{:S(2)}) %copy-start.1) | copy-done | bytes 262168
  3.3 0.0 copy-start.2
  3.3 0.9 %copy-done.2 = bf16[512,128]{1,0:T(8,128)(2,1)S(1)} copy-done((bf16[512,128]{1,0:T(8,128)(2,1)S(1)}, bf16[512,128]{1,0:T(8,128)(2,1)}, u32[]{:S(2)}) %copy-start.2) | copy-done | bytes 131096
  4.3 0.0 copy-start.3
  4.3 0.8 %copy-done.3 = bf16[128,256]{1,0:T(8,128)(2,1)S(1)} copy-done((bf16[128,256]{1,0:T(8,128)(2,1)S(1)}, bf16[128,256]{1,0:T(8,128)(2,1)}, u32[]{:S(2)}) %copy-start.3) | copy-done | bytes 65560
  5.1 33.8 %shard_map.94 = (bf16[512,256]{1,0:T(8,128)(2,1)S(1)}, bf16[4,128,128]{2,1,0:T(8,128)(2,1)S(1)}, f32[128,256]{1,0:T(8,128)S(1)}) custom-call(s32[1,1,19]{2,1,0:T(1,128)S(1)} %copy-done.4, s32[1,1,19]{2,1,0:T(1,128)S(1)} %copy-done.5, s32[1,1,4]{2,1,0:T(1,128)S(1)} %copy-done.6, bf16[4,128,128]{2,1,0:T(8,128)(2,1)S(1)} %bitcast.2, ...), custom_call_target="tpu_custom_call" | custom-call | tf_op jit(solution)/shard_map/pallas_call | solution.py:269
  38.9 0.7 %copy.13 = bf16[512,256]{1,0:T(8,128)(2,1)} copy(bf16[512,256]{1,0:T(8,128)(2,1)S(1)} %get-tuple-element.12) | data formatting | bytes 524288
  39.6 0.7 %copy.14 = bf16[512,128]{1,0:T(8,128)(2,1)} copy(bf16[512,128]{1,0:T(8,128)(2,1)S(1)} %bitcast.3) | data formatting | bytes 262144
  40.2 0.7 %copy.15 = f32[128,256]{1,0:T(8,128)} copy(f32[128,256]{1,0:T(8,128)S(1)} %get-tuple-element.14) | data formatting | bytes 262144
Async XLA Ops:
  0.6 0.7 %copy-start.6 = (s32[1,1,4]{2,1,0:T(1,128)S(1)}, s32[1,1,4]{2,1,0:T(1,128)}, u32[]{:S(2)}) copy-start(s32[1,1,4]{2,1,0:T(1,128)} %chosen_ref.1) | copy-start | bytes 52
  0.6 0.7 %copy-start.5 = (s32[1,1,19]{2,1,0:T(1,128)S(1)}, s32[1,1,19]{2,1,0:T(1,128)}, u32[]{:S(2)}) copy-start(s32[1,1,19]{2,1,0:T(1,128)} %sources_ref.1) | copy-start | bytes 232
  0.7 0.7 %copy-start.4 = (s32[1,1,19]{2,1,0:T(1,128)S(1)}, s32[1,1,19]{2,1,0:T(1,128)}, u32[]{:S(2)}) copy-start(s32[1,1,19]{2,1,0:T(1,128)} %rows_ref.1) | copy-start | bytes 232
  1.3 1.1 %copy-start = (bf16[1,1,19,128,128]{4,3,2,1,0:T(8,128)(2,1)S(1)}, bf16[1,1,19,128,128]{4,3,2,1,0:T(8,128)(2,1)}, u32[]{:S(2)}) copy-start(bf16[1,1,19,128,128]{4,3,2,1,0:T(8,128)(2,1)} %tiles_hbm.1) | copy-start | bytes 1867780
  2.4 0.9 %copy-start.1 = (bf16[512,256]{1,0:T(8,128)(2,1)S(1)}, bf16[512,256]{1,0:T(8,128)(2,1)}, u32[]{:S(2)}) copy-start(bf16[512,256]{1,0:T(8,128)(2,1)} %cot_hbm.1) | copy-start | bytes 786436
  3.3 0.9 %copy-start.2 = (bf16[512,128]{1,0:T(8,128)(2,1)S(1)}, bf16[512,128]{1,0:T(8,128)(2,1)}, u32[]{:S(2)}) copy-start(bf16[512,128]{1,0:T(8,128)(2,1)} %param.7) | copy-start | bytes 393220
  4.3 0.8 %copy-start.3 = (bf16[128,256]{1,0:T(8,128)(2,1)S(1)}, bf16[128,256]{1,0:T(8,128)(2,1)}, u32[]{:S(2)}) copy-start(bf16[128,256]{1,0:T(8,128)(2,1)} %weight_hbm.1) | copy-start | bytes 196612

commit v2 on v1

v2 whole, which is shorter than its diff:
```python
import functools
import math

import jax
import jax.numpy as jnp
from jax import lax
from jax.experimental import pallas as pl
from jax.experimental.pallas import tpu as pltpu
from jax.sharding import PartitionSpec as P

MESH = pl.DeviceIdType.MESH
BF16 = jnp.bfloat16
F32 = jnp.float32
DMA = pltpu.SemaphoreType.DMA


def each(low, high, step):
    if high - low <= 16:
        for i in range(low, high):
            step(i)
    else:
        lax.fori_loop(low, high, lambda i, c: (step(i), c)[1], 0)


def chain(keys, key_count, none):
    before = []
    for t, key in enumerate(keys):
        found = none
        for u in range(t):
            found = jnp.where(keys[u] == key, u, found)
        before.append(found)
    last = []
    for r in range(key_count):
        found = none
        for t, key in enumerate(keys):
            found = jnp.where(key == r, t, found)
        last.append(found)
    return before, last


def kernel(
    domains, members, sum_here, scale,
    rows_ref, sources_ref, chosen_ref, feat_hbm, weight_hbm, tiles_hbm, cot_hbm,
    act_hbm, fgrad_hbm, wgrad_hbm,
    feat, weight, tiles, tiles_t, cot, slots, outgoing, acc, last_ref, pair_out, pair_in, rs_out, rs_in,
    act, dom_h, ret_out, ret_in, fgrad, wown, wsend, wrecv, wzone, wzrecv, wgrad,
    local_sem, halo_send, halo_recv, pair_send, pair_recv, rs_send, rs_recv, ag_send, ag_recv,
    fw_send, fw_recv, ret_send, ret_recv, wb_send, wb_recv, wd_send, wd_recv,
    gb_send, gb_recv,
):
    own, size, width = feat.shape
    count = tiles.shape[0]
    d = lax.axis_index("dom")
    b = lax.axis_index("blk")
    pairs = members // 2
    chunks = rs_send.shape[1]
    span = own // chunks
    pair, side = lax.div(b, 2), lax.rem(b, 2)
    partner = b + 1 - 2 * side

    def dom_at(k):
        return lax.rem(d + k, domains)

    def blk_at(k):
        return lax.rem(b + k, members)

    def member(k, which):
        return 2 * lax.rem(pair + k, pairs) + which

    loads = [
        pltpu.make_async_copy(feat_hbm, feat, local_sem.at[0]),
        pltpu.make_async_copy(feat_hbm, slots.at[pl.ds(0, own)], local_sem.at[1]),
        pltpu.make_async_copy(tiles_hbm.at[0, 0], tiles, local_sem.at[2]),
        pltpu.make_async_copy(weight_hbm, weight, local_sem.at[3]),
        pltpu.make_async_copy(cot_hbm, cot, local_sem.at[4]),
    ]
    for load in loads:
        load.start()

    barrier = pltpu.get_barrier_semaphore()
    each(1, domains, lambda k: pl.semaphore_signal(
        barrier, inc=1, device_id={"dom": dom_at(k)}, device_id_type=MESH))
    each(1, members, lambda k: pl.semaphore_signal(
        barrier, inc=1, device_id={"blk": blk_at(k)}, device_id_type=MESH))

    loads[0].wait()

    def pick(k):
        outgoing[k - 1] = feat[jnp.minimum(chosen_ref[0, 0, dom_at(k)], own - 1)]

    each(1, domains, pick)
    pl.semaphore_wait(barrier, domains + members - 2)

    def halo(k):
        return pltpu.make_async_remote_copy(
            outgoing.at[k - 1], slots.at[own + d], halo_send.at[k - 1], halo_recv.at[k - 1],
            device_id={"dom": dom_at(k)}, device_id_type=MESH)

    def halo_in(k):
        return pltpu.make_async_remote_copy(
            outgoing.at[k - 1], slots.at[own + dom_at(domains - k)], halo_send.at[k - 1],
            halo_recv.at[k - 1], device_id={"dom": dom_at(k)}, device_id_type=MESH)

    each(1, domains, lambda k: halo(k).start())

    rows = [rows_ref[0, 0, t] for t in range(count)]
    sources = [sources_ref[0, 0, t] for t in range(count)]
    before, last = chain(rows, own * members, count)
    for r, value in enumerate(last):
        last_ref[r] = value
    acc[count] = jnp.zeros((size, width), F32)
    slots[own + d] = jnp.zeros((size, width), BF16)
    for load in loads[1:]:
        load.wait()
    each(1, domains, lambda k: halo_in(k).wait_recv())

    for t in range(count):
        product = jnp.dot(tiles[t], slots[sources[t]], preferred_element_type=F32)
        acc[t] = product + acc[before[t]]

    def remote(src, dst, send, recv, blk):
        return pltpu.make_async_remote_copy(
            src, dst, send, recv, device_id={"blk": blk}, device_id_type=MESH)

    def to_partner(k, c):
        part = pl.ds(c * span, span)
        return remote(pair_out.at[k, part], pair_in.at[k, part], pair_send.at[k, c],
                      pair_recv.at[k, c], partner)

    def across(k, c):
        part = pl.ds(c * span, span)
        return remote(rs_out.at[k - 1, part], rs_in.at[k - 1, part], rs_send.at[k - 1, c],
                      rs_recv.at[k - 1, c], member(k, side))

    order = [(k, c) for k in [*range(1, pairs), 0] for c in range(chunks)]
    for k, c in order:
        for s in range(c * span, (c + 1) * span):
            pair_out[k, s] = acc[last_ref[member(k, 1 - side) * own + s]].astype(BF16)
        to_partner(k, c).start()
    for k, c in order:
        if k:
            to_partner(k, c).wait_recv()
            for s in range(c * span, (c + 1) * span):
                rs_out[k - 1, s] = (
                    acc[last_ref[member(k, side) * own + s]] + pair_in[k, s].astype(F32)
                ).astype(BF16)
            across(k, c).start()

    before, last = chain(sources, own + domains, count)
    for t in range(count):
        tiles_t[t] = tiles[t].T

    def own_part(c):
        return dom_h.at[pl.ds(b * own + c * span, span)]

    def over(k, c):
        return remote(own_part(c), own_part(c), ag_send.at[k - 1, c], ag_recv.at[k - 1, c],
                      member(k, side))

    def held(k, c, which):
        return dom_h.at[pl.ds(member(pairs - k, which) * own + c * span, span)]

    def over_in(k, c):
        return remote(own_part(c), held(k, c, side), ag_send.at[k - 1, c], ag_recv.at[k - 1, c],
                      member(k, side))

    def forward(k, c):
        return remote(held(k, c, side), held(k, c, side), fw_send.at[k, c], fw_recv.at[k, c],
                      partner)

    def forward_in(k, c):
        return remote(held(k, c, side), held(k, c, 1 - side), fw_send.at[k, c], fw_recv.at[k, c],
                      partner)

    wpart = jnp.zeros(wown.shape, F32)
    later = []
    for c in range(chunks):
        to_partner(0, c).wait_recv()
        total = jnp.concatenate(
            [acc[last_ref[b * own + s]] + pair_in[0, s].astype(F32)
             for s in range(c * span, (c + 1) * span)], axis=0)
        for k in range(1, pairs):
            across(k, c).wait_recv()
            total += rs_in[k - 1, pl.ds(c * span, span)].reshape(span * size, width).astype(F32)
        gathered = total.astype(BF16)
        z = jnp.dot(gathered, weight[...], preferred_element_type=F32)
        sig = jax.nn.sigmoid(z)
        nodes = pl.ds(c * span * size, span * size)
        grad = (cot[nodes, :].astype(F32) * sig * (1.0 + z * (1.0 - sig))).astype(BF16)
        h = lax.dot_general(
            grad, weight[...], (((1,), (1,)), ((), ())), preferred_element_type=F32).astype(BF16)
        dom_h[pl.ds(b * own + c * span, span)] = h.reshape(span, size, width)
        for k in range(1, pairs):
            over(k, c).start()
        forward(0, c).start()
        act[nodes, :] = (z * sig).astype(BF16)
        later.append((gathered, grad))
    stores = [pltpu.make_async_copy(act, act_hbm, local_sem.at[5])]
    stores[0].start()
    for gathered, grad in later:
        wpart += lax.dot_general(
            gathered, grad, (((0,), (0,)), ((), ())), preferred_element_type=F32)
    wown[...] = wpart
    band = width // members
    mine = pl.ds(pl.multiple_of(b * band, 8), band)

    def wblk(m):
        rows_at = pl.ds(pl.multiple_of(blk_at(m) * band, 16), band)
        return remote(wsend.at[rows_at], wrecv.at[m - 1], wb_send.at[m - 1], wb_recv.at[m - 1],
                      blk_at(m))

    def wdom(k):
        return pltpu.make_async_remote_copy(
            wzone, wzrecv.at[k - 1], wd_send.at[k - 1], wd_recv.at[k - 1],
            device_id={"dom": dom_at(k)}, device_id_type=MESH)

    def gblk(m, who):
        at = pl.ds(pl.multiple_of(who * band, 8), band)
        return remote(wgrad.at[at], wgrad.at[at], gb_send.at[m - 1], gb_recv.at[m - 1], blk_at(m))

    if sum_here:
        wsend[...] = wpart.astype(BF16)
        for m in range(1, members):
            wblk(m).start()
    else:
        wgrad[...] = wpart * scale

    for c in range(chunks):
        for k in range(1, pairs):
            over_in(k, c).wait_recv()
            forward(k, c).start()
    for c in range(chunks):
        for k in range(pairs):
            forward_in(k, c).wait_recv()
    for t in range(count):
        product = jnp.dot(tiles_t[t], dom_h[rows[t]], preferred_element_type=F32)
        acc[t] = product + acc[before[t]]
    for s, value in enumerate(last):
        last_ref[s] = value

    if sum_here:
        summed = wown[mine, :]
        for m in range(1, members):
            wblk(m).wait_recv()
            summed += wrecv[m - 1].astype(F32)
        wzone[...] = summed.astype(BF16)
        each(1, domains, lambda k: wdom(k).start())

    def give_back(k):
        return pltpu.make_async_remote_copy(
            ret_out.at[k - 1], ret_in.at[k - 1], ret_send.at[k - 1], ret_recv.at[k - 1],
            device_id={"dom": dom_at(k)}, device_id_type=MESH)

    def give(k):
        ret_out[k - 1] = acc[last_ref[own + dom_at(k)]].astype(BF16)
        give_back(k).start()

    each(1, domains, give)

    if sum_here:
        summed = wzone[...].astype(F32)
        for k in range(1, domains):
            wdom(k).wait_recv()
            summed += wzrecv[k - 1].astype(F32)
        wgrad[mine, :] = summed * scale
        for m in range(1, members):
            gblk(m, b).start()

    for s in range(own):
        fgrad[s] = acc[last_ref[s]]

    def land(k):
        give_back(k).wait_recv()
        block = chosen_ref[0, 0, dom_at(domains - k)]
        value = ret_in[k - 1].astype(F32)
        for s in range(own):
            fgrad[s] += jnp.where(block == s, value, 0.0)

    each(1, domains, land)
    feat[...] = fgrad[...].astype(BF16)
    stores.append(pltpu.make_async_copy(feat, fgrad_hbm, local_sem.at[6]))
    stores[1].start()

    if sum_here:
        for m in range(1, members):
            gblk(m, blk_at(members - m)).wait_recv()
    stores.append(pltpu.make_async_copy(wgrad, wgrad_hbm, local_sem.at[7]))
    stores[2].start()

    each(1, domains, lambda k: halo(k).wait_send())
    each(1, domains, lambda k: give_back(k).wait_send())
    for c in range(chunks):
        for k in range(pairs):
            to_partner(k, c).wait_send()
            forward(k, c).wait_send()
            if k:
                across(k, c).wait_send()
                over(k, c).wait_send()
    if sum_here:
        each(1, domains, lambda k: wdom(k).wait_send())
        for m in range(1, members):
            wblk(m).wait_send()
            gblk(m, b).wait_send()
    for store in stores:
        store.wait()


def per_device(features, weight, tiles, tile_rows, tile_sources, send_blocks, cotangent):
    domains = lax.axis_size("dom")
    members = lax.axis_size("blk")
    peers = domains * members
    count, size = tiles.shape[2], tiles.shape[-1]
    own = features.shape[0] // size
    width, hidden = weight.shape
    nodes = own * size
    sum_here = width % (8 * peers) == 0
    scale = 1.0 / math.sqrt(nodes * peers)
    band = width // members
    zones = domains - 1 if sum_here and domains > 1 else 1
    halos = max(domains - 1, 1)
    others = max(members - 1, 1)
    pairs = members // 2
    far = max(pairs - 1, 1)
    chunks = 2 if own % 2 == 0 else 1
    vmem = pltpu.VMEM
    smem = pl.BlockSpec(memory_space=pltpu.SMEM)
    anywhere = pl.BlockSpec(memory_space=pl.ANY)
    activations, feature_grad, weight_grad = pl.pallas_call(
        functools.partial(kernel, domains, members, sum_here, scale),
        out_shape=(
            jax.ShapeDtypeStruct((nodes, hidden), BF16),
            jax.ShapeDtypeStruct((own, size, width), BF16),
            jax.ShapeDtypeStruct((width, hidden), F32),
        ),
        in_specs=[smem] * 3 + [anywhere] * 4,
        out_specs=(anywhere,) * 3,
        scratch_shapes=[
            vmem((own, size, width), BF16),
            vmem((width, hidden), BF16),
            vmem((count, size, size), BF16),
            vmem((count, size, size), BF16),
            vmem((nodes, hidden), BF16),
            vmem((own + domains, size, width), BF16),
            vmem((halos, size, width), BF16),
            vmem((count + 1, size, width), F32),
            pltpu.SMEM((max(own * members, own + domains),), jnp.int32),
            vmem((pairs, own, size, width), BF16),
            vmem((pairs, own, size, width), BF16),
            vmem((far, own, size, width), BF16),
            vmem((far, own, size, width), BF16),
            vmem((nodes, hidden), BF16),
            vmem((own * members, size, width), BF16),
            vmem((halos, size, width), BF16),
            vmem((halos, size, width), BF16),
            vmem((own, size, width), F32),
            vmem((width, hidden), F32),
            vmem((width, hidden), BF16),
            vmem((others, band, hidden), BF16),
            vmem((band, hidden), BF16),
            vmem((zones, band, hidden), BF16),
            vmem((width, hidden), F32),
            DMA((8,)),
            DMA((halos,)), DMA((halos,)),
            DMA((pairs, chunks)), DMA((pairs, chunks)),
            DMA((far, chunks)), DMA((far, chunks)),
            DMA((far, chunks)), DMA((far, chunks)),
            DMA((pairs, chunks)), DMA((pairs, chunks)),
            DMA((halos,)), DMA((halos,)),
            DMA((others,)), DMA((others,)),
            DMA((zones,)), DMA((zones,)),
            DMA((others,)), DMA((others,)),
        ],
        compiler_params=pltpu.CompilerParams(
            collective_id=0, has_side_effects=True, vmem_limit_bytes=55 * 1024 * 1024),
    )(tile_rows, tile_sources, send_blocks, features.reshape(own, size, width), weight, tiles, cotangent)
    if not sum_here:
        weight_grad = lax.psum(weight_grad, ("dom", "blk"))
    return activations, feature_grad.reshape(nodes, width), weight_grad


def solution(mesh):
    return jax.shard_map(
        per_device,
        mesh=mesh,
        in_specs=(
            P(("groups", "dom", "blk"), None),
            P(),
            P(("groups", "dom"), "blk", None, None, None),
            P(("groups", "dom"), "blk", None),
            P(("groups", "dom"), "blk", None),
            P(("groups", "dom"), "blk", None),
            P(("groups", "dom", "blk"), None),
        ),
        out_specs=(
            P(("groups", "dom", "blk"), None),
            P(("groups", "dom", "blk"), None),
            P("groups", None),
        ),
        check_vma=False,
    )
```

time: 41.2 us -> 33.9 us (0.82)
  Pallas kernels: 33.8 us -> 29.8 us
  local copies, waits for them, and re-layouts: 6.45 us -> 3.31 us
    pallas_call x1, Pallas kernels: 33.8 us -> 29.8 us  [per_device(): pl.pallas_call(functools.partial(kernel, domains, members, sum_here, scal...]
    unnamed x17 -> x7, local copies, waits for them, and re-layouts: 6.45 us -> 3.31 us
where the time goes in v2:
time: 33.9 us; the launch traced here: 33.8 us
  Pallas kernels  29.8 us (88%)
  local copies, waits for them, and re-layouts  3.31 us (10%)
  between operations  0.65 us (2%)
    pallas_call x1, Pallas kernels, per_device(): pl.pallas_call(functools.partial(kernel, domains, members, sum_here, scal...  29.8 us
    unnamed x7, local copies, waits for them, and re-layouts  3.31 us

profile of v2, /device:TPU:0, one launch (start us, length us, event | category | flops | bytes accessed | tf_op | source)
XLA Modules:
  0.0 33.8 jit_solution(10589722031247470282)
XLA Ops:
  0.6 29.8 %shard_map.94 = (bf16[512,256]{1,0:T(8,128)(2,1)}, bf16[4,128,128]{2,1,0:T(8,128)(2,1)}, f32[128,256]{1,0:T(8,128)}) custom-call(s32[1,1,19]{2,1,0:T(1,128)} %rows_ref.1, s32[1,1,19]{2,1,0:T(1,128)} %sources_ref.1, s32[1,1,4]{2,1,0:T(1,128)} %chosen_ref.1, bf16[4,128,128]{2,1,0:T(8,128)(2,1)} %bitcast.2, bf16[128,256]{1,0:T(8,128)(2,1)} %weight_hbm.1, ...), custom_call_target="tpu_custom_call" | custom-call | tf_op jit(solution)/shard_map/pallas_call | solution.py:328
  30.4 0.0 copy-start.1
  30.4 1.7 %copy.13 = bf16[512,256]{1,0:T(8,128)(2,1)} copy(bf16[512,256]{1,0:T(8,128)(2,1)} %get-tuple-element.12) | data formatting | bytes 524288
  32.2 0.0 copy-done.1
  32.2 0.0 copy-start
  32.2 0.7 %copy.14 = bf16[512,128]{1,0:T(8,128)(2,1)} copy(bf16[512,128]{1,0:T(8,128)(2,1)S(1)} %bitcast.3) | data formatting | bytes 262144
  32.8 0.3 copy-done
  33.1 0.7 %copy.15 = f32[128,256]{1,0:T(8,128)} copy(f32[128,256]{1,0:T(8,128)S(1)} %copy-done) | data formatting | bytes 262144
Async XLA Ops:
  30.4 1.7 %copy-start.1 = (bf16[4,128,128]{2,1,0:T(8,128)(2,1)S(1)}, bf16[4,128,128]{2,1,0:T(8,128)(2,1)}, u32[]{:S(2)}) copy-start(bf16[4,128,128]{2,1,0:T(8,128)(2,1)} %get-tuple-element.7) | copy-start | bytes 393220
  32.2 1.0 %copy-start = (f32[128,256]{1,0:T(8,128)S(1)}, f32[128,256]{1,0:T(8,128)}, u32[]{:S(2)}) copy-start(f32[128,256]{1,0:T(8,128)} %get-tuple-element.14) | copy-start | bytes 393220

commit v3 on v2

--- a/solution.py
+++ b/solution.py
@@ -41,9 +41,9 @@
 def kernel(
     domains, members, sum_here, scale,
     rows_ref, sources_ref, chosen_ref, feat_hbm, weight_hbm, tiles_hbm, cot_hbm,
-    act_hbm, fgrad_hbm, wgrad_hbm,
+    act, fgrad_out, wgrad_out,
     feat, weight, tiles, tiles_t, cot, slots, outgoing, acc, last_ref, pair_out, pair_in, rs_out, rs_in,
-    act, dom_h, ret_out, ret_in, fgrad, wown, wsend, wrecv, wzone, wzrecv, wgrad,
+    dom_h, ret_out, ret_in, fgrad, wown, wsend, wrecv, wzone, wzrecv, wgrad,
     local_sem, halo_send, halo_recv, pair_send, pair_recv, rs_send, rs_recv, ag_send, ag_recv,
     fw_send, fw_recv, ret_send, ret_recv, wb_send, wb_recv, wd_send, wd_recv,
     gb_send, gb_recv,
@@ -195,8 +195,6 @@
         forward(0, c).start()
         act[nodes, :] = (z * sig).astype(BF16)
         later.append((gathered, grad))
-    stores = [pltpu.make_async_copy(act, act_hbm, local_sem.at[5])]
-    stores[0].start()
     for gathered, grad in later:
         wpart += lax.dot_general(
             gathered, grad, (((0,), (0,)), ((), ())), preferred_element_type=F32)
@@ -229,6 +227,14 @@
         for k in range(1, pairs):
             over_in(k, c).wait_recv()
             forward(k, c).start()
+    if sum_here:
+        summed = wown[mine, :]
+        for m in range(1, members):
+            wblk(m).wait_recv()
+            summed += wrecv[m - 1].astype(F32)
+        wzone[...] = summed.astype(BF16)
+        each(1, domains, lambda k: wdom(k).start())
+
     for c in range(chunks):
         for k in range(pairs):
             forward_in(k, c).wait_recv()
@@ -238,14 +244,6 @@
     for s, value in enumerate(last):
         last_ref[s] = value
 
-    if sum_here:
-        summed = wown[mine, :]
-        for m in range(1, members):
-            wblk(m).wait_recv()
-            summed += wrecv[m - 1].astype(F32)
-        wzone[...] = summed.astype(BF16)
-        each(1, domains, lambda k: wdom(k).start())
-
     def give_back(k):
         return pltpu.make_async_remote_copy(
             ret_out.at[k - 1], ret_in.at[k - 1], ret_send.at[k - 1], ret_recv.at[k - 1],
@@ -277,15 +275,12 @@
             fgrad[s] += jnp.where(block == s, value, 0.0)
 
     each(1, domains, land)
-    feat[...] = fgrad[...].astype(BF16)
-    stores.append(pltpu.make_async_copy(feat, fgrad_hbm, local_sem.at[6]))
-    stores[1].start()
+    fgrad_out[...] = fgrad[...].astype(BF16)
 
     if sum_here:
         for m in range(1, members):
             gblk(m, blk_at(members - m)).wait_recv()
-    stores.append(pltpu.make_async_copy(wgrad, wgrad_hbm, local_sem.at[7]))
-    stores[2].start()
+    wgrad_out[...] = wgrad[...]
 
     each(1, domains, lambda k: halo(k).wait_send())
     each(1, domains, lambda k: give_back(k).wait_send())
@@ -301,8 +296,6 @@
         for m in range(1, members):
             wblk(m).wait_send()
             gblk(m, b).wait_send()
-    for store in stores:
-        store.wait()
 
 
 def per_device(features, weight, tiles, tile_rows, tile_sources, send_blocks, cotangent):
@@ -321,19 +314,19 @@
     others = max(members - 1, 1)
     pairs = members // 2
     far = max(pairs - 1, 1)
-    chunks = 2 if own % 2 == 0 else 1
+    chunks = own
     vmem = pltpu.VMEM
     smem = pl.BlockSpec(memory_space=pltpu.SMEM)
     anywhere = pl.BlockSpec(memory_space=pl.ANY)
     activations, feature_grad, weight_grad = pl.pallas_call(
         functools.partial(kernel, domains, members, sum_here, scale),
         out_shape=(
-            jax.ShapeDtypeStruct((nodes, hidden), BF16),
-            jax.ShapeDtypeStruct((own, size, width), BF16),
-            jax.ShapeDtypeStruct((width, hidden), F32),
+            vmem((nodes, hidden), BF16),
+            vmem((own, size, width), BF16),
+            vmem((width, hidden), F32),
         ),
         in_specs=[smem] * 3 + [anywhere] * 4,
-        out_specs=(anywhere,) * 3,
+        out_specs=(pl.BlockSpec(memory_space=pltpu.VMEM),) * 3,
         scratch_shapes=[
             vmem((own, size, width), BF16),
             vmem((width, hidden), BF16),
@@ -348,7 +341,6 @@
             vmem((pairs, own, size, width), BF16),
             vmem((far, own, size, width), BF16),
             vmem((far, own, size, width), BF16),
-            vmem((nodes, hidden), BF16),
             vmem((own * members, size, width), BF16),
             vmem((halos, size, width), BF16),
             vmem((halos, size, width), BF16),
@@ -359,7 +351,7 @@
             vmem((band, hidden), BF16),
             vmem((zones, band, hidden), BF16),
             vmem((width, hidden), F32),
-            DMA((8,)),
+            DMA((5,)),
             DMA((halos,)), DMA((halos,)),
             DMA((pairs, chunks)), DMA((pairs, chunks)),
             DMA((far, chunks)), DMA((far, chunks)),
@@ -371,7 +363,7 @@
             DMA((others,)), DMA((others,)),
         ],
         compiler_params=pltpu.CompilerParams(
-            collective_id=0, has_side_effects=True, vmem_limit_bytes=55 * 1024 * 1024),
+            collective_id=0, has_side_effects=True, vmem_limit_bytes=58 * 1024 * 1024),
     )(tile_rows, tile_sources, send_blocks, features.reshape(own, size, width), weight, tiles, cotangent)
     if not sum_here:
         weight_grad = lax.psum(weight_grad, ("dom", "blk"))

time: 33.9 us -> 30.5 us (0.90)
  Pallas kernels: 29.8 us -> 27.7 us
  local copies, waits for them, and re-layouts: 3.31 us -> 2.01 us
    pallas_call x1, Pallas kernels: 29.8 us -> 27.7 us  [per_device(): pl.pallas_call(functools.partial(kernel, domains, members, sum_here, scal...]
    unnamed x7 -> x3, local copies, waits for them, and re-layouts: 3.31 us -> 2.01 us
where the time goes in v3:
time: 30.5 us; the launch traced here: 30.4 us
  Pallas kernels  27.7 us (91%)
  local copies, waits for them, and re-layouts  2.01 us (7%)
  between operations  0.64 us (2%)
    pallas_call x1, Pallas kernels, per_device(): pl.pallas_call(functools.partial(kernel, domains, members, sum_here, scal...  27.7 us
    unnamed x3, local copies, waits for them, and re-layouts  2.01 us

profile of v3, /device:TPU:0, one launch (start us, length us, event | category | flops | bytes accessed | tf_op | source)
XLA Modules:
  0.0 30.4 jit_solution(3486427153968719065)
XLA Ops:
  0.6 27.7 %shard_map.94 = (bf16[512,256]{1,0:T(8,128)(2,1)S(1)}, bf16[4,128,128]{2,1,0:T(8,128)(2,1)S(1)}, f32[128,256]{1,0:T(8,128)S(1)}) custom-call(s32[1,1,19]{2,1,0:T(1,128)} %rows_ref.1, s32[1,1,19]{2,1,0:T(1,128)} %sources_ref.1, s32[1,1,4]{2,1,0:T(1,128)} %chosen_ref.1, bf16[4,128,128]{2,1,0:T(8,128)(2,1)} %bitcast.3, bf16[128,256]{1,0:T(8,128)(2,1)} %weight_hbm.1, ...), custom_call_target="tpu_custom_call" | custom-call | tf_op jit(solution)/shard_map/pallas_call | solution.py:321
  28.4 0.7 %copy.13 = bf16[512,256]{1,0:T(8,128)(2,1)} copy(bf16[512,256]{1,0:T(8,128)(2,1)S(1)} %get-tuple-element.9) | data formatting | bytes 524288
  29.1 0.7 %copy.14 = bf16[512,128]{1,0:T(8,128)(2,1)} copy(bf16[512,128]{1,0:T(8,128)(2,1)S(1)} %bitcast.2) | data formatting | bytes 262144
  29.7 0.7 %copy.15 = f32[128,256]{1,0:T(8,128)} copy(f32[128,256]{1,0:T(8,128)S(1)} %get-tuple-element.11) | data formatting | bytes 262144

commit v4 on v3

--- a/solution.py
+++ b/solution.py
@@ -101,7 +101,7 @@
             outgoing.at[k - 1], slots.at[own + dom_at(domains - k)], halo_send.at[k - 1],
             halo_recv.at[k - 1], device_id={"dom": dom_at(k)}, device_id_type=MESH)
 
-    each(1, domains, lambda k: halo(k).start())
+    each(1, domains, lambda k: halo(domains - k).start())
 
     rows = [rows_ref[0, 0, t] for t in range(count)]
     sources = [sources_ref[0, 0, t] for t in range(count)]
@@ -253,7 +253,7 @@
         ret_out[k - 1] = acc[last_ref[own + dom_at(k)]].astype(BF16)
         give_back(k).start()
 
-    each(1, domains, give)
+    each(1, domains, lambda k: give(domains - k))
 
     if sum_here:
         summed = wzone[...].astype(F32)

time: 30.5 us -> 29.9 us (0.980)
  Pallas kernels: 27.7 us -> 27.1 us
    pallas_call x1, Pallas kernels: 27.7 us -> 27.1 us  [per_device(): pl.pallas_call(functools.partial(kernel, domains, members, sum_here, scal...]
where the time goes in v4:
time: 29.9 us; the launch traced here: 29.8 us
  Pallas kernels  27.1 us (91%)
  local copies, waits for them, and re-layouts  2.01 us (7%)
  between operations  0.64 us (2%)
    pallas_call x1, Pallas kernels, per_device(): pl.pallas_call(functools.partial(kernel, domains, members, sum_here, scal...  27.1 us
    unnamed x3, local copies, waits for them, and re-layouts  2.01 us

profile of v4, /device:TPU:0, one launch (start us, length us, event | category | flops | bytes accessed | tf_op | source)
XLA Modules:
  0.0 29.8 jit_solution(1787106702341313894)
XLA Ops:
  0.6 27.1 %shard_map.94 = (bf16[512,256]{1,0:T(8,128)(2,1)S(1)}, bf16[4,128,128]{2,1,0:T(8,128)(2,1)S(1)}, f32[128,256]{1,0:T(8,128)S(1)}) custom-call(s32[1,1,19]{2,1,0:T(1,128)} %rows_ref.1, s32[1,1,19]{2,1,0:T(1,128)} %sources_ref.1, s32[1,1,4]{2,1,0:T(1,128)} %chosen_ref.1, bf16[4,128,128]{2,1,0:T(8,128)(2,1)} %bitcast.3, bf16[128,256]{1,0:T(8,128)(2,1)} %weight_hbm.1, ...), custom_call_target="tpu_custom_call" | custom-call | tf_op jit(solution)/shard_map/pallas_call | solution.py:321
  27.8 0.7 %copy.13 = bf16[512,256]{1,0:T(8,128)(2,1)} copy(bf16[512,256]{1,0:T(8,128)(2,1)S(1)} %get-tuple-element.9) | data formatting | bytes 524288
  28.5 0.7 %copy.14 = bf16[512,128]{1,0:T(8,128)(2,1)} copy(bf16[512,128]{1,0:T(8,128)(2,1)S(1)} %bitcast.2) | data formatting | bytes 262144
  29.1 0.7 %copy.15 = f32[128,256]{1,0:T(8,128)} copy(f32[128,256]{1,0:T(8,128)S(1)} %get-tuple-element.11) | data formatting | bytes 262144
